TPU v7x, 128 devices: a whole 4x4x4 slice. The times are simulated.
128 devices in a mesh: tm: 4 (over z), lat: 32 (over x, y, core).
Axes of the slice: x: 4, y: 4, z: 4, core: 2. Of those that a mesh axis runs over, the one named last changes fastest.
Arguments:
- forcing: float32 [4, 2, 137, 128, 128], P('tm', None, None, 'lat'), may hold values from -6 to 6
- coupling: float32 [137, 137], replicated, may hold values from -0.5 to 0.5
- diffusion: float32 [128, 128], P('lat'), may hold values from 0.02 to 0.12
- error_scale: float32 [137], replicated, may hold values from 0.3 to 3
- pick_cols: int32 [4, 32, 32, 16, 4], P('tm', 'lat'), may hold values from 0 to 511
- pick_weights: float32 [4, 32, 32, 16, 4], P('tm', 'lat'), may hold values from 0 to 1
- send_count: int32 [4, 32, 32], P('tm', 'lat'), may hold values from 1 to 16, 256 in all within a row
- jacobian: float32 [4, 32, 32, 16, 22, 137], P('tm', 'lat'), may hold values from -0.5 to 0.5
- obs_weight: float32 [4, 32, 32, 16, 22], P('tm', 'lat'), may hold values from 0.2 to 5
Outputs:
- gradient: float32 [4, 2, 137, 128, 128], P('tm', None, None, 'lat')
Inputs may be any that keep to these rules, and one draw needn't show every extreme that they name: The first send_count slots of each source band to each owner are used, the rest are empty; the counts of one source band in one sub-window sum to 256.
All inputs are finite; a program needn't handle non-finite values.
Results may differ from a plain program's by a relative error of at most 0.0001.
Values sent between devices are 32-bit elements; how exact they have to be, the bound alone decides.
A program may use at most 128 MiB of HBM per device.

v0:
```python
import functools
import jax
import jax.numpy as jnp
from jax import lax
from jax.experimental import pallas as pl
from jax.experimental.pallas import tpu as pltpu
from jax.sharding import PartitionSpec as P

F32 = jnp.float32
BF16 = jnp.bfloat16
MESH = pl.DeviceIdType.MESH
HIGHEST = lax.Precision.HIGHEST
TILE = 128
REGION = 512
FIELDS = 288
SPAN = 144
WINDOWS = 4

NN = ((1,), (0,))
NT = ((1,), (1,))


def dot(a, b, dims=NN, precision=None):
    return lax.dot_general(
        a, b, (dims, ((), ())), precision=precision, preferred_element_type=F32
    )


def halves(x):
    high = x.astype(BF16)
    return high, (x - high.astype(F32)).astype(BF16)


def thirds(x):
    high = x.astype(BF16)
    rest = x - high.astype(F32)
    middle = rest.astype(BF16)
    return high, middle, (rest - middle.astype(F32)).astype(BF16)


def dot3(a, b, dims=NN):
    return dot(a[0], b[0], dims) + (dot(a[0], b[1], dims) + dot(a[1], b[0], dims))


def band_column(i):
    return ((i >> 2) & 3) * 128 + (i >> 7) * 32 + ((i >> 4) & 7) * 4 + (i & 3)


def region_place(i):
    block = i >> 7
    row = ((i >> 2) & 3) + jnp.where(block == 1, -4, jnp.where(block == 2, 4, 0))
    lon = ((i >> 4) & 7) * 4 + (i & 3)
    edge = (i - 384) >> 4
    edge_row = ((i >> 2) & 3) + jnp.where(edge < 2, 0, jnp.where(edge < 4, -4, 4))
    edge_lon = (i & 3) + jnp.where((edge & 1) == 0, -4, 32)
    return jnp.where(i < 384, row, edge_row), jnp.where(i < 384, lon, edge_lon)


def step_matrix(bands, band, part, above, here, below):
    i = lax.broadcasted_iota(jnp.int32, (REGION, 128), 0)
    lane = lax.broadcasted_iota(jnp.int32, (REGION, 128), 1)
    row_i, lon_i = region_place(i)
    rows = jnp.zeros((REGION, 128), F32)
    for source, first in ((above, -4), (here, 0), (below, 4)):
        for k in range(4):
            rows = jnp.where(row_i == first + k, source[k : k + 1, :], rows)
    picked = lane == ((lon_i + 32 * part) & 127)
    spread = jnp.sum(jnp.where(picked, rows, 0.0), axis=1, keepdims=True)
    i1 = lax.broadcasted_iota(jnp.int32, (REGION, 1), 0)
    j1 = lax.broadcasted_iota(jnp.int32, (1, REGION), 1)
    row_a, lon_a = region_place(i1)
    row_b, lon_b = region_place(j1)
    last = 4 * bands - 4 * band
    ok_a = (row_a >= -4 * band) & (row_a < last) & (i1 < 480)
    ok_b = (row_b >= -4 * band) & (row_b < last) & (j1 < 480)
    spread = jnp.where(ok_a, spread, 0.0)
    one = jnp.where(ok_a, 1.0, 0.0)
    apart = jnp.abs(row_a - row_b) + jnp.abs(lon_a - lon_b)
    h = jnp.where(apart == 0, one - 4.0 * spread, jnp.where(apart == 1, spread, 0.0))
    return jnp.where(ok_b, h, 0.0)


EDGES = ((2, 1, 1, 1), (3, 0, 1, -1), (4, 1, -1, 1), (5, 0, -1, -1), (0, 1, 0, 1), (1, 0, 0, -1))


def whole_loop(bands, f, coupling, diff, picks, weights, counts, errors, jac, out,
               order, src, parts, region, own_edges, edges, ends, whole, dbuf, hmat, power,
               mixer, table, jbuf, jscaled, select, prof_out, prof_in, ret_out, ret_in,
               send_x, recv_x, send_h, recv_h, send_e, recv_e, send_d, recv_d,
               jsem, send_p, recv_p, send_r, recv_r):
    t, b = lax.axis_index("tm"), lax.axis_index("lat")
    channels, cap, levels = jac.shape[1:]
    mine = pl.ds(pl.multiple_of(t * TILE, TILE), TILE)

    def place(dt, db):
        return (lax.rem(t + dt + WINDOWS, WINDOWS), lax.rem(b + db + bands, bands))

    def band_at(d):
        return lax.rem(b + d + bands, bands)

    def remote(source, target, send, recv, device):
        return pltpu.make_async_remote_copy(
            src_ref=source, dst_ref=target, send_sem=send, recv_sem=recv,
            device_id=device, device_id_type=MESH,
        )

    def loop(first, last, body):
        def step(d, carry):
            body(d)
            return carry

        lax.fori_loop(first, last, step, 0)

    barrier = pltpu.get_barrier_semaphore()
    greeted = [(d, 0) for d in (1, 2, 3)] + [(d, s) for d in (-1, 1) for s in (-1, 1)]
    for dt, db in greeted:
        pl.semaphore_signal(barrier, inc=1, device_id=place(dt, db), device_id_type=MESH)
    loop(1, bands, lambda d: pl.semaphore_signal(
        barrier, inc=1, device_id=(t, band_at(d)), device_id_type=MESH))

    def jac_copy(q):
        return pltpu.make_async_copy(jac.at[q], jbuf.at[q], jsem.at[q])

    loop(0, bands, lambda q: jac_copy(q).start())

    place_i = band_column(lax.broadcasted_iota(jnp.int32, (REGION, 1), 0))
    column = lax.broadcasted_iota(jnp.int32, (1, REGION), 1)
    order[...] = (place_i == column).astype(F32).astype(BF16)
    for v in range(2):
        src[v * SPAN + 136 : (v + 1) * SPAN, :] = jnp.zeros((8, REGION), F32)
        for r in range(4):
            src[v * SPAN : v * SPAN + levels, r * 128 : (r + 1) * 128] = f[v, :, r, :]
    x = thirds(src[...])
    xt = dot(x[0], order[...], NT) + (dot(x[1], order[...], NT) + dot(x[2], order[...], NT))
    src[...] = xt

    pl.semaphore_wait(barrier, len(greeted) + bands - 1)

    spreads = [remote(diff, dbuf.at[k], send_d.at[k], recv_d.at[k], place(0, s))
               for k, s in ((0, 1), (1, -1))]
    for copy in spreads:
        copy.start()

    def scatter(s, source):
        copies = []
        for d in (1, 2, 3):
            to = lax.rem(t + d, WINDOWS)
            copy = remote(source.at[:, pl.ds(pl.multiple_of(to * TILE, TILE), TILE)],
                          parts.at[s, t], send_x.at[s, d], recv_x.at[s, t], (to, b))
            copy.start()
            copies.append(copy)
        parts[s, t] = source[:, mine]
        return copies

    started = scatter(0, src)

    for s in range(2):
        for w in range(WINDOWS):
            edges[s, w, 96:128, :] = jnp.zeros((32, 384), F32)
    eye = (lax.broadcasted_iota(jnp.int32, (levels, levels), 0)
           == lax.broadcasted_iota(jnp.int32, (levels, levels), 1)).astype(F32)
    mix = 0.8 * eye + 0.2 * coupling[...]
    twice = dot(mix, mix, precision=HIGHEST)
    power[...] = jnp.zeros((256, 256), F32)
    power[:levels, :levels] = dot(twice, twice, precision=HIGHEST)
    for s in range(2):
        full = power[...] if s == 0 else jnp.swapaxes(power[...], 0, 1)
        high, low = halves(full[:SPAN, :SPAN])
        mixer[s, 0] = high
        mixer[s, 1] = low

    for copy in spreads:
        copy.wait()
    hmat[...] = step_matrix(bands, b, t, dbuf[0], diff[...], dbuf[1])
    g = hmat[:TILE, :]
    for _ in range(3):
        g = dot(g, hmat[...], precision=HIGHEST)
    high, low = halves(jnp.swapaxes(g, 0, 1))
    table[0, 0] = high
    table[0, 1] = low

    edge_i = lax.broadcasted_iota(jnp.int32, (32, TILE), 0)
    edge_j = lax.broadcasted_iota(jnp.int32, (32, TILE), 1)
    edge_of = (edge_j == jnp.where(edge_i < 16, edge_i, edge_i + 96)).astype(F32).astype(BF16)

    def chain(s, windows, beside):
        before = None
        for w in windows:
            @pl.when(t != w)
            def _():
                remote(parts.at[s, w], parts.at[s, w], send_x.at[s, 0], recv_x.at[s, w],
                       (t, b)).wait_recv()

            state = parts[s, w]
            if before is not None:
                state = state + ends[s, before]
            high, low = halves(state)
            for v in range(2):
                rows = slice(v * SPAN, (v + 1) * SPAN)
                region[s, w, rows, :TILE] = dot3((mixer[s, 0], mixer[s, 1]), (high[rows], low[rows]))
            center = halves(region[s, w, :, :TILE])
            own_edges[s, w, :, :FIELDS] = dot(edge_of, center[0], NT) + dot(edge_of, center[1], NT)
            copies = []
            for at, side, db, dt in EDGES:
                copies.append(remote(own_edges.at[s, w, pl.ds(16 * side, 16)],
                                     edges.at[s, w, pl.ds(16 * at, 16)],
                                     send_h.at[s, w, at], recv_h.at[s, w, at], place(dt, db)))
            for k, db in ((6, 1), (7, -1)):
                copies.append(remote(region.at[s, w, :, pl.ds(0, TILE)],
                                     region.at[s, w, :, pl.ds((k - 5) * TILE, TILE)],
                                     send_h.at[s, w, k], recv_h.at[s, w, k], place(0, db)))
            for copy in copies:
                copy.start()
            part = dot3(center, (table[s, 0, :TILE], table[s, 1, :TILE]))
            if beside[w] is not None:
                beside[w]()
            for copy in copies:
                copy.wait_recv()
            started.extend(copies)
            region[s, w, :, 384:] = jnp.swapaxes(edges[s, w], 0, 1)[:FIELDS]
            ends[s, w] = part + dot3(halves(region[s, w, :, TILE:]),
                                     (table[s, 0, TILE:], table[s, 1, TILE:]))
            before = w

            @pl.when(t != w)
            def _():
                remote(ends.at[s, w], whole.at[s, :, mine], send_e.at[s, w], recv_e.at[s, t],
                       (w, b)).start()

            @pl.when(t == w)
            def _():
                whole[s, :, mine] = ends[s, w]

        for k in range(WINDOWS):
            @pl.when(t != k)
            def _():
                piece = whole.at[s, :, pl.ds(k * TILE, TILE)]
                remote(piece, piece, send_e.at[s, k], recv_e.at[s, k], (t, b)).wait_recv()
                remote(ends.at[s, k], ends.at[s, k], send_e.at[s, k], recv_e.at[s, k],
                       (t, b)).wait_send()

    slots = bands * cap

    def make_select():
        slot = lax.broadcasted_iota(jnp.int32, (slots, bands), 0)
        owner = lax.broadcasted_iota(jnp.int32, (slots, bands), 1)
        spread = (slot // cap == owner).astype(F32)
        near = picks.shape[1]
        row = lax.broadcasted_iota(jnp.int32, (slots, cap * near), 0)
        lane = lax.broadcasted_iota(jnp.int32, (slots, cap * near), 1)
        own = lane // near == row % cap
        chosen = jnp.zeros((slots, REGION), F32)
        col = jnp.concatenate([picks[c] for c in range(cap)], axis=0).astype(F32)
        wt = jnp.concatenate([jnp.where(counts[...] > c, weights[c], 0.0) for c in range(cap)], axis=0)
        col = dot(spread, col, NT, HIGHEST)
        wt = dot(spread, wt, NT, HIGHEST)
        at = band_column(lax.broadcasted_iota(jnp.int32, (1, REGION), 1)).astype(F32)
        for k in range(near):
            here = own & (lane % near == k)
            col_k = jnp.sum(jnp.where(here, col, 0.0), axis=1, keepdims=True)
            wt_k = jnp.sum(jnp.where(here, wt, 0.0), axis=1, keepdims=True)
            chosen += jnp.where(jnp.abs(col_k - at) < 0.5, wt_k, 0.0)
        high, low = halves(chosen)
        select[0] = high
        select[1] = low

    def scale_jac(first, last):
        lane = lax.broadcasted_iota(jnp.int32, (cap, bands), 1)

        def body(q):
            jac_copy(q).wait()
            for n in range(channels):
                scale = jnp.sum(jnp.where(lane == q, errors[n], 0.0), axis=1, keepdims=True)
                jscaled[q, n] = jbuf[q, n] * scale

        loop(first, last, body)

    def back_table():
        g = hmat[:, :TILE]
        for _ in range(3):
            g = dot(hmat[...], g, precision=HIGHEST)
        high, low = halves(g)
        table[1, 0] = high
        table[1, 1] = low

    chain(0, range(WINDOWS), [
        make_select, lambda: scale_jac(0, bands // 2), lambda: scale_jac(bands // 2, bands), back_table])

    def fold(x):
        count = x.shape[0] // cap
        x = x.reshape(count, cap, 384)
        last = x[:, :8, 256:] + pltpu.roll(x[:, 8:, 256:].reshape(count * 8, 128), 64, 1).reshape(count, 8, 128)
        return jnp.concatenate([x[:, :, :128], x[:, :, 128:256], last], axis=1)

    def unfold(x):
        count = x.shape[0]
        last = x[:, 2 * cap :]
        turned = pltpu.roll(last.reshape(count * 8, 128), 64, 1).reshape(count, 8, 128)
        last = jnp.concatenate([last, turned], axis=1)
        return jnp.concatenate([x[:, :cap], x[:, cap : 2 * cap], last], axis=2).reshape(count * cap, 384)

    high, low = halves(whole[0])
    spare = jnp.zeros((384 - FIELDS, REGION), BF16)
    state = (jnp.concatenate([high, spare], axis=0), jnp.concatenate([low, spare], axis=0))
    prof_out[...] = fold(dot3((select[0], select[1]), state, NT))

    def profile_copy(d):
        q = band_at(d)
        return remote(prof_out.at[q], prof_in.at[b], send_p.at[d], recv_p.at[d], (t, q))

    def profile_arrival(d):
        q = band_at(-d)
        return remote(prof_out.at[q], prof_in.at[q], send_p.at[d], recv_p.at[d], (t, q))

    def return_copy(d):
        q = band_at(-d)
        return remote(ret_out.at[q], ret_in.at[b], send_r.at[d], recv_r.at[d], (t, q))

    def return_arrival(d):
        q = band_at(d)
        return remote(ret_out.at[q], ret_in.at[q], send_r.at[d], recv_r.at[d], (t, q))

    loop(1, bands, lambda d: profile_copy(d).start())

    def work(q, packed):
        profile = unfold(packed[None])
        first = profile[:, :levels]
        second = pltpu.roll(profile[:, 128:], 256 - (SPAN - 128), 1)[:, :levels]
        sums = [jnp.zeros((cap, levels), F32)] * 2
        for n in range(channels):
            jn, jw = jbuf[q, n], jscaled[q, n]
            for v, p in enumerate((first, second)):
                hidden = jnp.sum(jn * p, axis=1, keepdims=True)
                sums[v] = sums[v] + jw * hidden
        spare = jnp.zeros((cap, 256 - levels), F32)
        one = jnp.concatenate([sums[0], spare], axis=1)
        two = pltpu.roll(jnp.concatenate([sums[1], spare], axis=1), SPAN - 128, 1)
        back = jnp.concatenate([one[:, :128], one[:, 128:] + two[:, :128], two[:, 128:]], axis=1)
        return fold(back)[0]

    ret_in[b] = work(b, prof_out[b])

    def serve(d):
        q = band_at(-d)
        profile_arrival(d).wait_recv()
        ret_out[q] = work(q, prof_in[q])
        return_copy(d).start()

    loop(1, bands, serve)
    loop(1, bands, lambda d: return_arrival(d).wait_recv())
    back = halves(jnp.swapaxes(unfold(ret_in[...]), 0, 1)[:FIELDS])
    src2 = whole.at[2]
    src2[...] = dot3(back, (select[0], select[1]))
    started += scatter(1, src2)
    chain(1, range(WINDOWS - 1, -1, -1), [None] * WINDOWS)
    x = thirds(whole[1])
    out[...] = dot(x[0], order[...]) + (dot(x[1], order[...]) + dot(x[2], order[...]))

    for copy in started:
        copy.wait_send()

    def drain(d):
        return_copy(d).wait_send()
        profile_copy(d).wait_send()

    loop(1, bands, drain)


def run(bands, f, coupling, diff, picks, weights, counts, errors, jac):
    vmem = pl.BlockSpec(memory_space=pltpu.VMEM)
    dma = pltpu.SemaphoreType.DMA
    slots = bands * jac.shape[2]
    packed = pltpu.VMEM((bands, 40, 128), F32)
    return pl.pallas_call(
        functools.partial(whole_loop, bands),
        out_shape=jax.ShapeDtypeStruct((FIELDS, REGION), F32),
        in_specs=[vmem] * 7 + [pl.BlockSpec(memory_space=pl.ANY)],
        out_specs=vmem,
        scratch_shapes=[
            pltpu.VMEM((REGION, REGION), BF16),
            pltpu.VMEM((FIELDS, REGION), F32),
            pltpu.VMEM((2, WINDOWS, FIELDS, TILE), F32),
            pltpu.VMEM((2, WINDOWS, FIELDS, REGION), F32),
            pltpu.VMEM((2, WINDOWS, 32, 384), F32),
            pltpu.VMEM((2, WINDOWS, 128, 384), F32),
            pltpu.VMEM((2, WINDOWS, FIELDS, TILE), F32),
            pltpu.VMEM((3, FIELDS, REGION), F32),
            pltpu.VMEM((2, 4, 128), F32),
            pltpu.VMEM((REGION, REGION), F32),
            pltpu.VMEM((256, 256), F32),
            pltpu.VMEM((2, 2, SPAN, SPAN), BF16),
            pltpu.VMEM((2, 2, REGION, TILE), BF16),
            pltpu.VMEM(jac.shape, F32),
            pltpu.VMEM(jac.shape, F32),
            pltpu.VMEM((2, slots, REGION), BF16),
            packed, packed, packed, packed,
            dma((2, 4)), dma((2, 4)),
            dma((2, 4, 8)), dma((2, 4, 8)),
            dma((2, 4)), dma((2, 4)),
            dma((2,)), dma((2,)),
            dma((bands,)), dma((bands,)), dma((bands,)), dma((bands,)), dma((bands,)),
        ],
        compiler_params=pltpu.CompilerParams(
            collective_id=0, has_side_effects=True, vmem_limit_bytes=56 * 1024 * 1024,
        ),
        name="inner_loop",
    )(f, coupling, diff, picks, weights, counts, errors, jac)


def shards(forcing, coupling, diffusion, error_scale, pick_cols, pick_weights,
           send_count, jacobian, obs_weight):
    own = forcing[0]
    lanczos, levels, rows, longitudes = own.shape
    adjoint = run(
        lax.axis_size("lat"), own, coupling, diffusion,
        jnp.transpose(pick_cols[0, 0], (1, 2, 0)),
        jnp.transpose(pick_weights[0, 0], (1, 2, 0)),
        send_count[0],
        jnp.transpose(obs_weight[0, 0], (2, 1, 0)),
        jnp.transpose(jacobian[0, 0], (0, 2, 1, 3)),
    )
    adjoint = adjoint.reshape(lanczos, SPAN, rows, longitudes)[:, :levels]
    return (adjoint + error_scale[None, :, None, None] * own)[None]


def solution(mesh):
    return jax.shard_map(
        shards,
        mesh=mesh,
        in_specs=(
            P("tm", None, None, "lat", None),
            P(),
            P("lat", None),
            P(),
            P("tm", "lat", None, None, None),
            P("tm", "lat", None, None, None),
            P("tm", "lat", None),
            P("tm", "lat", None, None, None, None),
            P("tm", "lat", None, None, None),
        ),
        out_specs=P("tm", None, None, "lat", None),
        check_vma=False,
    )
```

profile of v0, /device:TPU:0, one launch (start us, length us, event | category | flops | bytes accessed | tf_op | source)
XLA Modules:
  0.0 129.7 jit_solution(14801220835353890088)
XLA Ops:
  0.0 0.0 copy-start
  0.0 0.0 copy-start.1
  0.0 127.4 %inner_loop.1 = f32[288,512]{1,0:T(8,128)} custom-call(f32[2,137,4,128]{3,2,1,0:T(4,128)} %bitcast.18, f32[137,137]{1,0:T(8,128)} %coupling.1, f32[4,128]{1,0:T(4,128)} %diff.1, s32[16,4,32]{2,1,0:T(4,128)} %bitcast.20, f32[16,4,32]{2,1,0:T(4,128)} %bitcast.21, s32[1,32]{1,0:T(1,128)} %bitcast.22, f32[22,16,32]{2,1,0:T(8,128)} %bitcast.19, ...), custom_call_target="tpu_custom_call" | custom-call | tf_op jit(solution)/shard_map/inner_loop/pallas_call | solution.py:374
  127.4 1.3 reshape.4
  128.6 0.0 copy-done
  128.6 0.0 copy-done.1
  128.6 1.0 fusion
Async XLA Ops:
  0.0 128.6 %copy-start = (f32[1,2,137,4,128]{4,3,2,1,0:T(4,128)S(1)}, f32[1,2,137,4,128]{4,3,2,1,0:T(4,128)}, u32[]{:S(2)}) copy-start(f32[1,2,137,4,128]{4,3,2,1,0:T(4,128)} %param.9) | copy-start | bytes 1683460
  0.0 128.6 %copy-start.1 = (f32[137]{0:T(256)S(1)}, f32[137]{0:T(256)}, u32[]{:S(2)}) copy-start(f32[137]{0:T(256)} %param.12) | copy-start | bytes 1648
where the time goes:
time: 130 us
  Pallas kernels  127 us (98%)
    pallas_call x1, Pallas kernels, run(): pl.pallas_call(functools.partial(whole_loop, bands), out_shape=jax.ShapeD...  127 us

commit v1 on v0

--- a/solution.py
+++ b/solution.py
@@ -127,12 +127,11 @@
     column = lax.broadcasted_iota(jnp.int32, (1, REGION), 1)
     order[...] = (place_i == column).astype(F32).astype(BF16)
     for v in range(2):
-        src[v * SPAN + 136 : (v + 1) * SPAN, :] = jnp.zeros((8, REGION), F32)
+        src[v, 136:, :] = jnp.zeros((8, REGION), F32)
         for r in range(4):
-            src[v * SPAN : v * SPAN + levels, r * 128 : (r + 1) * 128] = f[v, :, r, :]
-    x = thirds(src[...])
-    xt = dot(x[0], order[...], NT) + (dot(x[1], order[...], NT) + dot(x[2], order[...], NT))
-    src[...] = xt
+            src[v, :levels, r * 128 : (r + 1) * 128] = f[v, :, r, :]
+        x = thirds(src[v])
+        src[v] = dot(x[0], order[...], NT) + (dot(x[1], order[...], NT) + dot(x[2], order[...], NT))
 
     pl.semaphore_wait(barrier, len(greeted) + bands - 1)
 
@@ -141,22 +140,31 @@
     for copy in spreads:
         copy.start()
 
-    def scatter(s, source):
-        copies = []
-        for d in (1, 2, 3):
-            to = lax.rem(t + d, WINDOWS)
-            copy = remote(source.at[:, pl.ds(pl.multiple_of(to * TILE, TILE), TILE)],
-                          parts.at[s, t], send_x.at[s, d], recv_x.at[s, t], (to, b))
-            copy.start()
-            copies.append(copy)
-        parts[s, t] = source[:, mine]
-        return copies
-
-    started = scatter(0, src)
+    started = []
+
+    def scatter_copy(s, source, d, v):
+        to = lax.rem(t + d, WINDOWS)
+        return remote(source.at[v, :, pl.ds(pl.multiple_of(to * TILE, TILE), TILE)],
+                      parts.at[s, t, v], send_x.at[s, v, d], recv_x.at[s, t, v], (to, b))
+
+    def scatter(s, source, w):
+        @pl.when(t == w)
+        def _():
+            for v in range(2):
+                for d in (2, 1, 3):
+                    scatter_copy(s, source, d, v).start()
+
+    def keep_own(s, source):
+        for v in range(2):
+            parts[s, t, v] = source[v, :, mine]
+
+    scatter(0, src, 0)
+    keep_own(0, src)
 
     for s in range(2):
         for w in range(WINDOWS):
-            edges[s, w, 96:128, :] = jnp.zeros((32, 384), F32)
+            for v in range(2):
+                edges[s, w, v, 96:, :] = jnp.zeros((32, 256), F32)
     eye = (lax.broadcasted_iota(jnp.int32, (levels, levels), 0)
            == lax.broadcasted_iota(jnp.int32, (levels, levels), 1)).astype(F32)
     mix = 0.8 * eye + 0.2 * coupling[...]
@@ -183,61 +191,72 @@
     edge_j = lax.broadcasted_iota(jnp.int32, (32, TILE), 1)
     edge_of = (edge_j == jnp.where(edge_i < 16, edge_i, edge_i + 96)).astype(F32).astype(BF16)
 
-    def chain(s, windows, beside):
-        before = None
-        for w in windows:
-            @pl.when(t != w)
-            def _():
-                remote(parts.at[s, w], parts.at[s, w], send_x.at[s, 0], recv_x.at[s, w],
-                       (t, b)).wait_recv()
-
-            state = parts[s, w]
-            if before is not None:
-                state = state + ends[s, before]
-            high, low = halves(state)
+    def halo_copies(s, w, v):
+        copies = []
+        for at, side, db, dt in EDGES:
+            copies.append(remote(own_edges.at[s, w, v, pl.ds(16 * side, 16)],
+                                 edges.at[s, w, v, pl.ds(16 * at, 16)],
+                                 send_h.at[s, w, v, at], recv_h.at[s, w, v, at], place(dt, db)))
+        for k, db in ((1, 1), (2, -1)):
+            copies.append(remote(region.at[s, w, v, :, pl.ds(0, TILE)],
+                                 region.at[s, w, v, :, pl.ds(k * TILE, TILE)],
+                                 send_h.at[s, w, v, 5 + k], recv_h.at[s, w, v, 5 + k], place(0, db)))
+        return copies
+
+    def send_halo(s, w, before, v):
+        @pl.when(t != w)
+        def _():
+            remote(parts.at[s, w, v], parts.at[s, w, v], send_x.at[s, v, 0], recv_x.at[s, w, v],
+                   (t, b)).wait_recv()
+
+        state = parts[s, w, v]
+        if before is not None:
+            state = state + ends[s, before, v]
+        mixed = dot3((mixer[s, 0], mixer[s, 1]), halves(state))
+        center = halves(mixed)
+        own_edges[s, w, v, :, :SPAN] = dot(edge_of, center[0], NT) + dot(edge_of, center[1], NT)
+        region[s, w, v, :, :TILE] = mixed
+        copies = halo_copies(s, w, v)
+        for copy in copies:
+            copy.start()
+        started.extend(copies)
+        ends[s, w, v] = dot3(center, (table[s, 0, :TILE], table[s, 1, :TILE]))
+
+    def receive_halo(s, w, v):
+        for copy in halo_copies(s, w, v):
+            copy.wait_recv()
+        region[s, w, v, :, 384:] = jnp.swapaxes(edges[s, w, v], 0, 1)[:SPAN]
+        ends[s, w, v] += dot3(halves(region[s, w, v, :, TILE:]),
+                              (table[s, 0, TILE:], table[s, 1, TILE:]))
+
+        @pl.when(t != w)
+        def _():
+            remote(ends.at[s, w, v], whole.at[s, v, :, mine], send_e.at[s, w, v],
+                   recv_e.at[s, t, v], (w, b)).start()
+
+        @pl.when(t == w)
+        def _():
+            whole[s, v, :, mine] = ends[s, w, v]
+
+    def chain(s, windows, source, beside):
+        for v in range(2):
+            send_halo(s, windows[0], None, v)
+        for k, w in enumerate(windows):
+            if k < WINDOWS - 1:
+                scatter(s, source, windows[k + 1])
+            if beside[k] is not None:
+                beside[k]()
             for v in range(2):
-                rows = slice(v * SPAN, (v + 1) * SPAN)
-                region[s, w, rows, :TILE] = dot3((mixer[s, 0], mixer[s, 1]), (high[rows], low[rows]))
-            center = halves(region[s, w, :, :TILE])
-            own_edges[s, w, :, :FIELDS] = dot(edge_of, center[0], NT) + dot(edge_of, center[1], NT)
-            copies = []
-            for at, side, db, dt in EDGES:
-                copies.append(remote(own_edges.at[s, w, pl.ds(16 * side, 16)],
-                                     edges.at[s, w, pl.ds(16 * at, 16)],
-                                     send_h.at[s, w, at], recv_h.at[s, w, at], place(dt, db)))
-            for k, db in ((6, 1), (7, -1)):
-                copies.append(remote(region.at[s, w, :, pl.ds(0, TILE)],
-                                     region.at[s, w, :, pl.ds((k - 5) * TILE, TILE)],
-                                     send_h.at[s, w, k], recv_h.at[s, w, k], place(0, db)))
-            for copy in copies:
-                copy.start()
-            part = dot3(center, (table[s, 0, :TILE], table[s, 1, :TILE]))
-            if beside[w] is not None:
-                beside[w]()
-            for copy in copies:
-                copy.wait_recv()
-            started.extend(copies)
-            region[s, w, :, 384:] = jnp.swapaxes(edges[s, w], 0, 1)[:FIELDS]
-            ends[s, w] = part + dot3(halves(region[s, w, :, TILE:]),
-                                     (table[s, 0, TILE:], table[s, 1, TILE:]))
-            before = w
-
-            @pl.when(t != w)
-            def _():
-                remote(ends.at[s, w], whole.at[s, :, mine], send_e.at[s, w], recv_e.at[s, t],
-                       (w, b)).start()
-
-            @pl.when(t == w)
-            def _():
-                whole[s, :, mine] = ends[s, w]
-
+                receive_halo(s, w, v)
+                if k < WINDOWS - 1:
+                    send_halo(s, windows[k + 1], w, v)
+
+    def collect(s, v):
         for k in range(WINDOWS):
             @pl.when(t != k)
             def _():
-                piece = whole.at[s, :, pl.ds(k * TILE, TILE)]
-                remote(piece, piece, send_e.at[s, k], recv_e.at[s, k], (t, b)).wait_recv()
-                remote(ends.at[s, k], ends.at[s, k], send_e.at[s, k], recv_e.at[s, k],
-                       (t, b)).wait_send()
+                piece = whole.at[s, v, :, pl.ds(k * TILE, TILE)]
+                remote(piece, piece, send_e.at[s, k, v], recv_e.at[s, k, v], (t, b)).wait_recv()
 
     slots = bands * cap
 
@@ -283,7 +302,7 @@
         table[1, 0] = high
         table[1, 1] = low
 
-    chain(0, range(WINDOWS), [
+    chain(0, (0, 1, 2, 3), src, [
         make_select, lambda: scale_jac(0, bands // 2), lambda: scale_jac(bands // 2, bands), back_table])
 
     def fold(x):
@@ -299,7 +318,9 @@
         last = jnp.concatenate([last, turned], axis=1)
         return jnp.concatenate([x[:, :cap], x[:, cap : 2 * cap], last], axis=2).reshape(count * cap, 384)
 
-    high, low = halves(whole[0])
+    collect(0, 0)
+    collect(0, 1)
+    high, low = halves(whole[0].reshape(FIELDS, REGION))
     spare = jnp.zeros((384 - FIELDS, REGION), BF16)
     state = (jnp.concatenate([high, spare], axis=0), jnp.concatenate([low, spare], axis=0))
     prof_out[...] = fold(dot3((select[0], select[1]), state, NT))
@@ -349,13 +370,27 @@
     loop(1, bands, serve)
     loop(1, bands, lambda d: return_arrival(d).wait_recv())
     back = halves(jnp.swapaxes(unfold(ret_in[...]), 0, 1)[:FIELDS])
-    src2 = whole.at[2]
-    src2[...] = dot3(back, (select[0], select[1]))
-    started += scatter(1, src2)
-    chain(1, range(WINDOWS - 1, -1, -1), [None] * WINDOWS)
-    x = thirds(whole[1])
-    out[...] = dot(x[0], order[...]) + (dot(x[1], order[...]) + dot(x[2], order[...]))
-
+    seen = whole.at[2]
+    seen[...] = dot3(back, (select[0], select[1])).reshape(2, SPAN, REGION)
+    scatter(1, seen, 3)
+    keep_own(1, seen)
+    chain(1, (3, 2, 1, 0), seen, [None] * WINDOWS)
+    for v in range(2):
+        collect(1, v)
+        x = thirds(whole[1, v])
+        end = dot(x[0], order[...]) + (dot(x[1], order[...]) + dot(x[2], order[...]))
+        for r in range(4):
+            out[v, :, r, :] = end[:levels, r * 128 : (r + 1) * 128]
+
+    for s, source in ((0, src), (1, seen)):
+        for v in range(2):
+            for d in (1, 2, 3):
+                scatter_copy(s, source, d, v).wait_send()
+            for k in range(WINDOWS):
+                @pl.when(t != k)
+                def _():
+                    remote(ends.at[s, k, v], whole.at[s, v, :, mine], send_e.at[s, k, v],
+                           recv_e.at[s, t, v], (k, b)).wait_send()
     for copy in started:
         copy.wait_send()
 
@@ -373,18 +408,18 @@
     packed = pltpu.VMEM((bands, 40, 128), F32)
     return pl.pallas_call(
         functools.partial(whole_loop, bands),
-        out_shape=jax.ShapeDtypeStruct((FIELDS, REGION), F32),
+        out_shape=jax.ShapeDtypeStruct(f.shape, F32),
         in_specs=[vmem] * 7 + [pl.BlockSpec(memory_space=pl.ANY)],
         out_specs=vmem,
         scratch_shapes=[
             pltpu.VMEM((REGION, REGION), BF16),
-            pltpu.VMEM((FIELDS, REGION), F32),
-            pltpu.VMEM((2, WINDOWS, FIELDS, TILE), F32),
-            pltpu.VMEM((2, WINDOWS, FIELDS, REGION), F32),
-            pltpu.VMEM((2, WINDOWS, 32, 384), F32),
-            pltpu.VMEM((2, WINDOWS, 128, 384), F32),
-            pltpu.VMEM((2, WINDOWS, FIELDS, TILE), F32),
-            pltpu.VMEM((3, FIELDS, REGION), F32),
+            pltpu.VMEM((2, SPAN, REGION), F32),
+            pltpu.VMEM((2, WINDOWS, 2, SPAN, TILE), F32),
+            pltpu.VMEM((2, WINDOWS, 2, SPAN, REGION), F32),
+            pltpu.VMEM((2, WINDOWS, 2, 32, 256), F32),
+            pltpu.VMEM((2, WINDOWS, 2, 128, 256), F32),
+            pltpu.VMEM((2, WINDOWS, 2, SPAN, TILE), F32),
+            pltpu.VMEM((3, 2, SPAN, REGION), F32),
             pltpu.VMEM((2, 4, 128), F32),
             pltpu.VMEM((REGION, REGION), F32),
             pltpu.VMEM((256, 256), F32),
@@ -394,9 +429,9 @@
             pltpu.VMEM(jac.shape, F32),
             pltpu.VMEM((2, slots, REGION), BF16),
             packed, packed, packed, packed,
-            dma((2, 4)), dma((2, 4)),
-            dma((2, 4, 8)), dma((2, 4, 8)),
-            dma((2, 4)), dma((2, 4)),
+            dma((2, 2, 4)), dma((2, 4, 2)),
+            dma((2, 4, 2, 8)), dma((2, 4, 2, 8)),
+            dma((2, 4, 2)), dma((2, 4, 2)),
             dma((2,)), dma((2,)),
             dma((bands,)), dma((bands,)), dma((bands,)), dma((bands,)), dma((bands,)),
         ],
@@ -410,7 +445,6 @@
 def shards(forcing, coupling, diffusion, error_scale, pick_cols, pick_weights,
            send_count, jacobian, obs_weight):
     own = forcing[0]
-    lanczos, levels, rows, longitudes = own.shape
     adjoint = run(
         lax.axis_size("lat"), own, coupling, diffusion,
         jnp.transpose(pick_cols[0, 0], (1, 2, 0)),
@@ -419,7 +453,6 @@
         jnp.transpose(obs_weight[0, 0], (2, 1, 0)),
         jnp.transpose(jacobian[0, 0], (0, 2, 1, 3)),
     )
-    adjoint = adjoint.reshape(lanczos, SPAN, rows, longitudes)[:, :levels]
     return (adjoint + error_scale[None, :, None, None] * own)[None]
 
 

time: 130 us -> 138 us (1.062)
  Pallas kernels: 127 us -> 135 us
    pallas_call x1, Pallas kernels: 127 us -> 135 us  [run(): pl.pallas_call(functools.partial(whole_loop, bands), out_shape=jax.ShapeD...]
where the time goes in v1:
time: 138 us; the launch traced here: 137 us
  Pallas kernels  135 us (98%)
  other arithmetic  2.08 us (2%)
    pallas_call x1, Pallas kernels, run(): pl.pallas_call(functools.partial(whole_loop, bands), out_shape=jax.ShapeD...  135 us

profile of v1, /device:TPU:0, one launch (start us, length us, event | category | flops | bytes accessed | tf_op | source)
XLA Modules:
  0.0 137.4 jit_solution(5377348022097143236)
XLA Ops:
  0.0 0.0 copy-start
  0.0 0.0 copy-start.1
  0.0 135.3 %inner_loop.1 = f32[2,137,4,128]{3,2,1,0:T(4,128)} custom-call(f32[2,137,4,128]{3,2,1,0:T(4,128)} %bitcast.18, f32[137,137]{1,0:T(8,128)} %coupling.1, f32[4,128]{1,0:T(4,128)} %diff.1, s32[16,4,32]{2,1,0:T(4,128)} %bitcast.20, f32[16,4,32]{2,1,0:T(4,128)} %bitcast.21, s32[1,32]{1,0:T(1,128)} %bitcast.22, f32[22,16,32]{2,1,0:T(8,128)} %bitcast.19, ...), custom_call_target="tpu_custom_call" | custom-call | tf_op jit(solution)/shard_map/inner_loop/pallas_call | solution.py:409
  135.3 0.0 copy-done
  135.3 0.0 copy-done.1
  135.3 2.1 %add_bitcast_fusion = f32[1,2,137,4,128]{4,3,2,1,0:T(4,128)} fusion(f32[2,137,4,128]{3,2,1,0:T(4,128)} %inner_loop.1, f32[137]{0:T(256)S(1)} %copy-done.1, f32[1,2,137,4,128]{4,3,2,1,0:T(4,128)S(1)} %copy-done), kind=kLoop, calls=%fused_computation | loop fusion | flops 280576 | bytes 1684004 | tf_op jit(solution)/shard_map/broadcast_in_dim | solution.py:456
Async XLA Ops:
  0.0 135.3 %copy-start = (f32[1,2,137,4,128]{4,3,2,1,0:T(4,128)S(1)}, f32[1,2,137,4,128]{4,3,2,1,0:T(4,128)}, u32[]{:S(2)}) copy-start(f32[1,2,137,4,128]{4,3,2,1,0:T(4,128)} %param.9) | copy-start | bytes 1683460
  0.0 135.3 %copy-start.1 = (f32[137]{0:T(256)S(1)}, f32[137]{0:T(256)}, u32[]{:S(2)}) copy-start(f32[137]{0:T(256)} %param.12) | copy-start | bytes 1648

commit v2 on v1

--- a/solution.py
+++ b/solution.py
@@ -83,8 +83,8 @@
 EDGES = ((2, 1, 1, 1), (3, 0, 1, -1), (4, 1, -1, 1), (5, 0, -1, -1), (0, 1, 0, 1), (1, 0, 0, -1))
 
 
-def whole_loop(bands, f, coupling, diff, picks, weights, counts, errors, jac, out,
-               order, src, parts, region, own_edges, edges, ends, whole, dbuf, hmat, power,
+def whole_loop(bands, f_hbm, coupling_hbm, diff_hbm, picks_hbm, weights_hbm, counts_hbm, errors_hbm, jac, out,
+               f, coupling, diff, picks, weights, counts, errors, fetched, order, src, parts, region, own_edges, edges, ends, whole, dbuf, hmat, power,
                mixer, table, jbuf, jscaled, select, prof_out, prof_in, ret_out, ret_in,
                send_x, recv_x, send_h, recv_h, send_e, recv_e, send_d, recv_d,
                jsem, send_p, recv_p, send_r, recv_r):
@@ -118,6 +118,13 @@
     loop(1, bands, lambda d: pl.semaphore_signal(
         barrier, inc=1, device_id=(t, band_at(d)), device_id_type=MESH))
 
+    fetches = []
+    for k, (source, target) in enumerate((
+            (f_hbm, f), (coupling_hbm, coupling), (diff_hbm, diff), (picks_hbm, picks),
+            (weights_hbm, weights), (counts_hbm, counts), (errors_hbm, errors))):
+        fetches.append(pltpu.make_async_copy(source, target, fetched.at[k]))
+        fetches[-1].start()
+
     def jac_copy(q):
         return pltpu.make_async_copy(jac.at[q], jbuf.at[q], jsem.at[q])
 
@@ -126,6 +133,8 @@
     place_i = band_column(lax.broadcasted_iota(jnp.int32, (REGION, 1), 0))
     column = lax.broadcasted_iota(jnp.int32, (1, REGION), 1)
     order[...] = (place_i == column).astype(F32).astype(BF16)
+    for copy in fetches:
+        copy.wait()
     for v in range(2):
         src[v, 136:, :] = jnp.zeros((8, REGION), F32)
         for r in range(4):
@@ -147,19 +156,14 @@
         return remote(source.at[v, :, pl.ds(pl.multiple_of(to * TILE, TILE), TILE)],
                       parts.at[s, t, v], send_x.at[s, v, d], recv_x.at[s, t, v], (to, b))
 
-    def scatter(s, source, w):
-        @pl.when(t == w)
-        def _():
-            for v in range(2):
-                for d in (2, 1, 3):
-                    scatter_copy(s, source, d, v).start()
-
-    def keep_own(s, source):
+    def scatter(s, source):
+        for v in range(2):
+            for d in (2, 1, 3):
+                scatter_copy(s, source, d, v).start()
         for v in range(2):
             parts[s, t, v] = source[v, :, mine]
 
-    scatter(0, src, 0)
-    keep_own(0, src)
+    scatter(0, src)
 
     for s in range(2):
         for w in range(WINDOWS):
@@ -229,6 +233,7 @@
         ends[s, w, v] += dot3(halves(region[s, w, v, :, TILE:]),
                               (table[s, 0, TILE:], table[s, 1, TILE:]))
 
+    def send_end(s, w, v):
         @pl.when(t != w)
         def _():
             remote(ends.at[s, w, v], whole.at[s, v, :, mine], send_e.at[s, w, v],
@@ -238,18 +243,21 @@
         def _():
             whole[s, v, :, mine] = ends[s, w, v]
 
-    def chain(s, windows, source, beside):
+    def chain(s, windows, beside):
         for v in range(2):
             send_halo(s, windows[0], None, v)
         for k, w in enumerate(windows):
-            if k < WINDOWS - 1:
-                scatter(s, source, windows[k + 1])
             if beside[k] is not None:
                 beside[k]()
             for v in range(2):
                 receive_halo(s, w, v)
                 if k < WINDOWS - 1:
                     send_halo(s, windows[k + 1], w, v)
+                else:
+                    send_end(s, w, v)
+        for w in windows[-2::-1]:
+            for v in range(2):
+                send_end(s, w, v)
 
     def collect(s, v):
         for k in range(WINDOWS):
@@ -302,7 +310,7 @@
         table[1, 0] = high
         table[1, 1] = low
 
-    chain(0, (0, 1, 2, 3), src, [
+    chain(0, (0, 1, 2, 3), [
         make_select, lambda: scale_jac(0, bands // 2), lambda: scale_jac(bands // 2, bands), back_table])
 
     def fold(x):
@@ -325,23 +333,39 @@
     state = (jnp.concatenate([high, spare], axis=0), jnp.concatenate([low, spare], axis=0))
     prof_out[...] = fold(dot3((select[0], select[1]), state, NT))
 
+    across = min(4, bands // 2)
+    down = bands // (2 * across)
+
+    def far_first(j, size):
+        if size == 4:
+            return lax.rem(2 + 3 * j + 3 * (j * (j - 1) // 2), 4)
+        return size - 1 - j
+
+    def partner(d, sign):
+        core = lax.rem(b + d + 1, 2)
+        dy = far_first(lax.rem(d // 2, across), across)
+        dx = far_first(d // (2 * across), down)
+        y = lax.rem(lax.rem(b // 2, across) + sign * dy + across, across)
+        x = lax.rem(b // (2 * across) + sign * dx + down, down)
+        return (x * across + y) * 2 + core
+
     def profile_copy(d):
-        q = band_at(d)
+        q = partner(d, 1)
         return remote(prof_out.at[q], prof_in.at[b], send_p.at[d], recv_p.at[d], (t, q))
 
     def profile_arrival(d):
-        q = band_at(-d)
+        q = partner(d, -1)
         return remote(prof_out.at[q], prof_in.at[q], send_p.at[d], recv_p.at[d], (t, q))
 
     def return_copy(d):
-        q = band_at(-d)
+        q = partner(d, -1)
         return remote(ret_out.at[q], ret_in.at[b], send_r.at[d], recv_r.at[d], (t, q))
 
     def return_arrival(d):
-        q = band_at(d)
+        q = partner(d, 1)
         return remote(ret_out.at[q], ret_in.at[q], send_r.at[d], recv_r.at[d], (t, q))
 
-    loop(1, bands, lambda d: profile_copy(d).start())
+    loop(0, bands - 1, lambda d: profile_copy(d).start())
 
     def work(q, packed):
         profile = unfold(packed[None])
@@ -362,19 +386,18 @@
     ret_in[b] = work(b, prof_out[b])
 
     def serve(d):
-        q = band_at(-d)
+        q = partner(d, -1)
         profile_arrival(d).wait_recv()
         ret_out[q] = work(q, prof_in[q])
         return_copy(d).start()
 
-    loop(1, bands, serve)
-    loop(1, bands, lambda d: return_arrival(d).wait_recv())
+    loop(0, bands - 1, serve)
+    loop(0, bands - 1, lambda d: return_arrival(d).wait_recv())
     back = halves(jnp.swapaxes(unfold(ret_in[...]), 0, 1)[:FIELDS])
     seen = whole.at[2]
     seen[...] = dot3(back, (select[0], select[1])).reshape(2, SPAN, REGION)
-    scatter(1, seen, 3)
-    keep_own(1, seen)
-    chain(1, (3, 2, 1, 0), seen, [None] * WINDOWS)
+    scatter(1, seen)
+    chain(1, (3, 2, 1, 0), [None] * WINDOWS)
     for v in range(2):
         collect(1, v)
         x = thirds(whole[1, v])
@@ -398,7 +421,7 @@
         return_copy(d).wait_send()
         profile_copy(d).wait_send()
 
-    loop(1, bands, drain)
+    loop(0, bands - 1, drain)
 
 
 def run(bands, f, coupling, diff, picks, weights, counts, errors, jac):
@@ -409,9 +432,13 @@
     return pl.pallas_call(
         functools.partial(whole_loop, bands),
         out_shape=jax.ShapeDtypeStruct(f.shape, F32),
-        in_specs=[vmem] * 7 + [pl.BlockSpec(memory_space=pl.ANY)],
+        in_specs=[pl.BlockSpec(memory_space=pl.ANY)] * 8,
         out_specs=vmem,
         scratch_shapes=[
+            pltpu.VMEM(x.shape, x.dtype)
+            for x in (f, coupling, diff, picks, weights, counts, errors)
+        ] + [
+            dma((7,)),
             pltpu.VMEM((REGION, REGION), BF16),
             pltpu.VMEM((2, SPAN, REGION), F32),
             pltpu.VMEM((2, WINDOWS, 2, SPAN, TILE), F32),

time: 138 us -> 114 us (0.83)
  Pallas kernels: 135 us -> 112 us
    pallas_call x1, Pallas kernels: 135 us -> 112 us  [run(): pl.pallas_call(functools.partial(whole_loop, bands), out_shape=jax.ShapeD...]
where the time goes in v2:
time: 114 us
  Pallas kernels  112 us (98%)
  other arithmetic  2.08 us (2%)
    pallas_call x1, Pallas kernels, run(): pl.pallas_call(functools.partial(whole_loop, bands), out_shape=jax.ShapeD...  112 us

profile of v2, /device:TPU:0, one launch (start us, length us, event | category | flops | bytes accessed | tf_op | source)
XLA Modules:
  0.0 114.1 jit_solution(10019078388384754581)
XLA Ops:
  0.0 0.0 copy-start
  0.0 0.0 copy-start.1
  0.0 112.0 %inner_loop.1 = f32[2,137,4,128]{3,2,1,0:T(4,128)} custom-call(f32[2,137,4,128]{3,2,1,0:T(4,128)} %bitcast.18, f32[137,137]{1,0:T(8,128)} %coupling_hbm.1, f32[4,128]{1,0:T(4,128)} %diff_hbm.1, s32[16,4,32]{2,1,0:T(4,128)} %bitcast.20, f32[16,4,32]{2,1,0:T(4,128)} %bitcast.21, s32[1,32]{1,0:T(1,128)} %bitcast.22, f32[22,16,32]{2,1,0:T(8,128)} %bitcast.19, ...), custom_call_target="tpu_custom_call" | custom-call | tf_op jit(solution)/shard_map/inner_loop/pallas_call | solution.py:432
  112.0 0.0 copy-done
  112.0 0.0 copy-done.1
  112.0 2.1 %add_bitcast_fusion = f32[1,2,137,4,128]{4,3,2,1,0:T(4,128)} fusion(f32[2,137,4,128]{3,2,1,0:T(4,128)} %inner_loop.1, f32[137]{0:T(256)S(1)} %copy-done.1, f32[1,2,137,4,128]{4,3,2,1,0:T(4,128)S(1)} %copy-done), kind=kLoop, calls=%fused_computation | loop fusion | flops 280576 | bytes 1684004 | tf_op jit(solution)/shard_map/broadcast_in_dim | solution.py:483
Async XLA Ops:
  0.0 112.0 %copy-start = (f32[1,2,137,4,128]{4,3,2,1,0:T(4,128)S(1)}, f32[1,2,137,4,128]{4,3,2,1,0:T(4,128)}, u32[]{:S(2)}) copy-start(f32[1,2,137,4,128]{4,3,2,1,0:T(4,128)} %param.9) | copy-start | bytes 1683460
  0.0 112.0 %copy-start.1 = (f32[137]{0:T(256)S(1)}, f32[137]{0:T(256)}, u32[]{:S(2)}) copy-start(f32[137]{0:T(256)} %param.12) | copy-start | bytes 1648

commit v3 on v2

--- a/solution.py
+++ b/solution.py
@@ -46,14 +46,36 @@
     return ((i >> 2) & 3) * 128 + (i >> 7) * 32 + ((i >> 4) & 7) * 4 + (i & 3)
 
 
+def corner_cell(j):
+    down = jnp.where(j < 3, 1, jnp.where(j < 5, 2, 3))
+    return down, jnp.where(j < 3, j + 1, jnp.where(j < 5, j - 2, j - 4))
+
+
 def region_place(i):
     block = i >> 7
     row = ((i >> 2) & 3) + jnp.where(block == 1, -4, jnp.where(block == 2, 4, 0))
     lon = ((i >> 4) & 7) * 4 + (i & 3)
-    edge = (i - 384) >> 4
-    edge_row = ((i >> 2) & 3) + jnp.where(edge < 2, 0, jnp.where(edge < 4, -4, 4))
-    edge_lon = (i & 3) + jnp.where((edge & 1) == 0, -4, 32)
-    return jnp.where(i < 384, row, edge_row), jnp.where(i < 384, lon, edge_lon)
+    k = i - 384
+    side_lon = (i & 3) + jnp.where(k < 16, -4, 32)
+    corner = (k - 32) >> 3
+    dr, dl = corner_cell(k & 7)
+    corner_row = jnp.where(corner < 2, -dr, 3 + dr)
+    corner_lon = jnp.where((corner & 1) == 0, -dl, 31 + dl)
+    row = jnp.where(i < 416, jnp.where(i < 384, row, (i >> 2) & 3), corner_row)
+    return row, jnp.where(i < 384, lon, jnp.where(i < 416, side_lon, corner_lon))
+
+
+def region_used(i):
+    return (i < 416) | ((i < 448) & ((i & 7) < 6))
+
+
+def edge_column(i):
+    side = jnp.where(i < 16, i, i + 96)
+    corner = (i - 32) >> 3
+    dr, dl = corner_cell(i & 7)
+    row = jnp.where(corner < 2, 4 - dr, dr - 1)
+    lon = jnp.where((corner & 1) == 0, 32 - dl, dl - 1)
+    return jnp.where(i < 32, side, (lon >> 2) * 16 + row * 4 + (lon & 3))
 
 
 def step_matrix(bands, band, part, above, here, below):
@@ -71,8 +93,8 @@
     row_a, lon_a = region_place(i1)
     row_b, lon_b = region_place(j1)
     last = 4 * bands - 4 * band
-    ok_a = (row_a >= -4 * band) & (row_a < last) & (i1 < 480)
-    ok_b = (row_b >= -4 * band) & (row_b < last) & (j1 < 480)
+    ok_a = (row_a >= -4 * band) & (row_a < last) & region_used(i1)
+    ok_b = (row_b >= -4 * band) & (row_b < last) & region_used(j1)
     spread = jnp.where(ok_a, spread, 0.0)
     one = jnp.where(ok_a, 1.0, 0.0)
     apart = jnp.abs(row_a - row_b) + jnp.abs(lon_a - lon_b)
@@ -80,7 +102,14 @@
     return jnp.where(ok_b, h, 0.0)
 
 
-EDGES = ((2, 1, 1, 1), (3, 0, 1, -1), (4, 1, -1, 1), (5, 0, -1, -1), (0, 1, 0, 1), (1, 0, 0, -1))
+EDGES = (
+    (32, 32, 8, 1, 1),
+    (40, 40, 8, 1, -1),
+    (48, 48, 8, -1, 1),
+    (56, 56, 8, -1, -1),
+    (0, 16, 16, 0, 1),
+    (16, 0, 16, 0, -1),
+)
 
 
 def whole_loop(bands, f_hbm, coupling_hbm, diff_hbm, picks_hbm, weights_hbm, counts_hbm, errors_hbm, jac, out,
@@ -168,7 +197,7 @@
     for s in range(2):
         for w in range(WINDOWS):
             for v in range(2):
-                edges[s, w, v, 96:, :] = jnp.zeros((32, 256), F32)
+                edges[s, w, v, 64:, :] = jnp.zeros((64, 256), F32)
     eye = (lax.broadcasted_iota(jnp.int32, (levels, levels), 0)
            == lax.broadcasted_iota(jnp.int32, (levels, levels), 1)).astype(F32)
     mix = 0.8 * eye + 0.2 * coupling[...]
@@ -181,26 +210,27 @@
         mixer[s, 0] = high
         mixer[s, 1] = low
 
-    for copy in spreads:
-        copy.wait()
-    hmat[...] = step_matrix(bands, b, t, dbuf[0], diff[...], dbuf[1])
-    g = hmat[:TILE, :]
-    for _ in range(3):
-        g = dot(g, hmat[...], precision=HIGHEST)
-    high, low = halves(jnp.swapaxes(g, 0, 1))
-    table[0, 0] = high
-    table[0, 1] = low
-
-    edge_i = lax.broadcasted_iota(jnp.int32, (32, TILE), 0)
-    edge_j = lax.broadcasted_iota(jnp.int32, (32, TILE), 1)
-    edge_of = (edge_j == jnp.where(edge_i < 16, edge_i, edge_i + 96)).astype(F32).astype(BF16)
+    def ahead_table():
+        for copy in spreads:
+            copy.wait()
+        hmat[...] = step_matrix(bands, b, t, dbuf[0], diff[...], dbuf[1])
+        g = hmat[:TILE, :]
+        for _ in range(3):
+            g = dot(g, hmat[...], precision=HIGHEST)
+        high, low = halves(jnp.swapaxes(g, 0, 1))
+        table[0, 0] = high
+        table[0, 1] = low
+
+    edge_i = edge_column(lax.broadcasted_iota(jnp.int32, (64, TILE), 0))
+    edge_j = lax.broadcasted_iota(jnp.int32, (64, TILE), 1)
+    edge_of = (edge_j == edge_i).astype(F32).astype(BF16)
 
     def halo_copies(s, w, v):
         copies = []
-        for at, side, db, dt in EDGES:
-            copies.append(remote(own_edges.at[s, w, v, pl.ds(16 * side, 16)],
-                                 edges.at[s, w, v, pl.ds(16 * at, 16)],
-                                 send_h.at[s, w, v, at], recv_h.at[s, w, v, at], place(dt, db)))
+        for k, (at, start, size, db, dt) in enumerate(EDGES):
+            copies.append(remote(own_edges.at[s, w, v, pl.ds(start, size)],
+                                 edges.at[s, w, v, pl.ds(at, size)],
+                                 send_h.at[s, w, v, k], recv_h.at[s, w, v, k], place(dt, db)))
         for k, db in ((1, 1), (2, -1)):
             copies.append(remote(region.at[s, w, v, :, pl.ds(0, TILE)],
                                  region.at[s, w, v, :, pl.ds(k * TILE, TILE)],
@@ -224,14 +254,12 @@
         for copy in copies:
             copy.start()
         started.extend(copies)
-        ends[s, w, v] = dot3(center, (table[s, 0, :TILE], table[s, 1, :TILE]))
 
     def receive_halo(s, w, v):
         for copy in halo_copies(s, w, v):
             copy.wait_recv()
         region[s, w, v, :, 384:] = jnp.swapaxes(edges[s, w, v], 0, 1)[:SPAN]
-        ends[s, w, v] += dot3(halves(region[s, w, v, :, TILE:]),
-                              (table[s, 0, TILE:], table[s, 1, TILE:]))
+        ends[s, w, v] = dot3(halves(region[s, w, v]), (table[s, 0], table[s, 1]))
 
     def send_end(s, w, v):
         @pl.when(t != w)
@@ -311,7 +339,7 @@
         table[1, 1] = low
 
     chain(0, (0, 1, 2, 3), [
-        make_select, lambda: scale_jac(0, bands // 2), lambda: scale_jac(bands // 2, bands), back_table])
+        ahead_table, make_select, lambda: scale_jac(0, bands), back_table])
 
     def fold(x):
         count = x.shape[0] // cap
@@ -365,7 +393,8 @@
         q = partner(d, 1)
         return remote(ret_out.at[q], ret_in.at[q], send_r.at[d], recv_r.at[d], (t, q))
 
-    loop(0, bands - 1, lambda d: profile_copy(d).start())
+    profile_copy(bands - 2).start()
+    loop(0, bands - 2, lambda d: profile_copy(d).start())
 
     def work(q, packed):
         profile = unfold(packed[None])
@@ -391,7 +420,8 @@
         ret_out[q] = work(q, prof_in[q])
         return_copy(d).start()
 
-    loop(0, bands - 1, serve)
+    serve(bands - 2)
+    loop(0, bands - 2, serve)
     loop(0, bands - 1, lambda d: return_arrival(d).wait_recv())
     back = halves(jnp.swapaxes(unfold(ret_in[...]), 0, 1)[:FIELDS])
     seen = whole.at[2]
@@ -443,7 +473,7 @@
             pltpu.VMEM((2, SPAN, REGION), F32),
             pltpu.VMEM((2, WINDOWS, 2, SPAN, TILE), F32),
             pltpu.VMEM((2, WINDOWS, 2, SPAN, REGION), F32),
-            pltpu.VMEM((2, WINDOWS, 2, 32, 256), F32),
+            pltpu.VMEM((2, WINDOWS, 2, 64, 256), F32),
             pltpu.VMEM((2, WINDOWS, 2, 128, 256), F32),
             pltpu.VMEM((2, WINDOWS, 2, SPAN, TILE), F32),
             pltpu.VMEM((3, 2, SPAN, REGION), F32),

time: 114 us -> 113 us (level)
    pallas_call x1, Pallas kernels: 112 us -> 111 us  [run(): pl.pallas_call(functools.partial(whole_loop, bands), out_shape=jax.ShapeD...]
where the time goes in v3:
time: 113 us
  Pallas kernels  111 us (98%)
  other arithmetic  2.08 us (2%)
    pallas_call x1, Pallas kernels, run(): pl.pallas_call(functools.partial(whole_loop, bands), out_shape=jax.ShapeD...  111 us

profile of v3, /device:TPU:0, one launch (start us, length us, event | category | flops | bytes accessed | tf_op | source)
XLA Modules:
  0.0 112.6 jit_solution(7754547412887112454)
XLA Ops:
  0.0 0.0 copy-start
  0.0 0.0 copy-start.1
  0.0 110.5 %inner_loop.1 = f32[2,137,4,128]{3,2,1,0:T(4,128)} custom-call(f32[2,137,4,128]{3,2,1,0:T(4,128)} %bitcast.18, f32[137,137]{1,0:T(8,128)} %coupling_hbm.1, f32[4,128]{1,0:T(4,128)} %diff_hbm.1, s32[16,4,32]{2,1,0:T(4,128)} %bitcast.20, f32[16,4,32]{2,1,0:T(4,128)} %bitcast.21, s32[1,32]{1,0:T(1,128)} %bitcast.22, f32[22,16,32]{2,1,0:T(8,128)} %bitcast.19, ...), custom_call_target="tpu_custom_call" | custom-call | tf_op jit(solution)/shard_map/inner_loop/pallas_call | solution.py:462
  110.5 0.0 copy-done
  110.5 0.0 copy-done.1
  110.5 2.1 %add_bitcast_fusion = f32[1,2,137,4,128]{4,3,2,1,0:T(4,128)} fusion(f32[2,137,4,128]{3,2,1,0:T(4,128)} %inner_loop.1, f32[137]{0:T(256)S(1)} %copy-done.1, f32[1,2,137,4,128]{4,3,2,1,0:T(4,128)S(1)} %copy-done), kind=kLoop, calls=%fused_computation | loop fusion | flops 280576 | bytes 1684004 | tf_op jit(solution)/shard_map/broadcast_in_dim | solution.py:513
Async XLA Ops:
  0.0 110.5 %copy-start = (f32[1,2,137,4,128]{4,3,2,1,0:T(4,128)S(1)}, f32[1,2,137,4,128]{4,3,2,1,0:T(4,128)}, u32[]{:S(2)}) copy-start(f32[1,2,137,4,128]{4,3,2,1,0:T(4,128)} %param.9) | copy-start | bytes 1683460
  0.0 110.5 %copy-start.1 = (f32[137]{0:T(256)S(1)}, f32[137]{0:T(256)}, u32[]{:S(2)}) copy-start(f32[137]{0:T(256)} %param.12) | copy-start | bytes 1648

commit v4 on v3

--- a/solution.py
+++ b/solution.py
@@ -112,8 +112,8 @@
 )
 
 
-def whole_loop(bands, f_hbm, coupling_hbm, diff_hbm, picks_hbm, weights_hbm, counts_hbm, errors_hbm, jac, out,
-               f, coupling, diff, picks, weights, counts, errors, fetched, order, src, parts, region, own_edges, edges, ends, whole, dbuf, hmat, power,
+def whole_loop(bands, f_hbm, coupling_hbm, diff_hbm, picks_hbm, weights_hbm, counts_hbm, errors_hbm,
+               balance_hbm, jac, out, f, coupling, diff, picks, weights, counts, errors, balance, fetched, order, src, parts, region, own_edges, edges, ends, whole, dbuf, hmat, power,
                mixer, table, jbuf, jscaled, select, prof_out, prof_in, ret_out, ret_in,
                send_x, recv_x, send_h, recv_h, send_e, recv_e, send_d, recv_d,
                jsem, send_p, recv_p, send_r, recv_r):
@@ -150,7 +150,8 @@
     fetches = []
     for k, (source, target) in enumerate((
             (f_hbm, f), (coupling_hbm, coupling), (diff_hbm, diff), (picks_hbm, picks),
-            (weights_hbm, weights), (counts_hbm, counts), (errors_hbm, errors))):
+            (weights_hbm, weights), (counts_hbm, counts), (errors_hbm, errors),
+            (balance_hbm, balance))):
         fetches.append(pltpu.make_async_copy(source, target, fetched.at[k]))
         fetches[-1].start()
 
@@ -201,6 +202,7 @@
     eye = (lax.broadcasted_iota(jnp.int32, (levels, levels), 0)
            == lax.broadcasted_iota(jnp.int32, (levels, levels), 1)).astype(F32)
     mix = 0.8 * eye + 0.2 * coupling[...]
+    scale = jnp.sum(eye * balance[...], axis=1, keepdims=True)
     twice = dot(mix, mix, precision=HIGHEST)
     power[...] = jnp.zeros((256, 256), F32)
     power[:levels, :levels] = dot(twice, twice, precision=HIGHEST)
@@ -433,7 +435,7 @@
         x = thirds(whole[1, v])
         end = dot(x[0], order[...]) + (dot(x[1], order[...]) + dot(x[2], order[...]))
         for r in range(4):
-            out[v, :, r, :] = end[:levels, r * 128 : (r + 1) * 128]
+            out[v, :, r, :] = end[:levels, r * 128 : (r + 1) * 128] + scale * f[v, :, r, :]
 
     for s, source in ((0, src), (1, seen)):
         for v in range(2):
@@ -454,7 +456,7 @@
     loop(0, bands - 1, drain)
 
 
-def run(bands, f, coupling, diff, picks, weights, counts, errors, jac):
+def run(bands, f, coupling, diff, picks, weights, counts, errors, balance, jac):
     vmem = pl.BlockSpec(memory_space=pltpu.VMEM)
     dma = pltpu.SemaphoreType.DMA
     slots = bands * jac.shape[2]
@@ -462,13 +464,13 @@
     return pl.pallas_call(
         functools.partial(whole_loop, bands),
         out_shape=jax.ShapeDtypeStruct(f.shape, F32),
-        in_specs=[pl.BlockSpec(memory_space=pl.ANY)] * 8,
+        in_specs=[pl.BlockSpec(memory_space=pl.ANY)] * 9,
         out_specs=vmem,
         scratch_shapes=[
             pltpu.VMEM(x.shape, x.dtype)
-            for x in (f, coupling, diff, picks, weights, counts, errors)
+            for x in (f, coupling, diff, picks, weights, counts, errors, balance)
         ] + [
-            dma((7,)),
+            dma((8,)),
             pltpu.VMEM((REGION, REGION), BF16),
             pltpu.VMEM((2, SPAN, REGION), F32),
             pltpu.VMEM((2, WINDOWS, 2, SPAN, TILE), F32),
@@ -496,21 +498,22 @@
             collective_id=0, has_side_effects=True, vmem_limit_bytes=56 * 1024 * 1024,
         ),
         name="inner_loop",
-    )(f, coupling, diff, picks, weights, counts, errors, jac)
+    )(f, coupling, diff, picks, weights, counts, errors, balance, jac)
 
 
 def shards(forcing, coupling, diffusion, error_scale, pick_cols, pick_weights,
            send_count, jacobian, obs_weight):
     own = forcing[0]
-    adjoint = run(
+    gradient = run(
         lax.axis_size("lat"), own, coupling, diffusion,
         jnp.transpose(pick_cols[0, 0], (1, 2, 0)),
         jnp.transpose(pick_weights[0, 0], (1, 2, 0)),
         send_count[0],
         jnp.transpose(obs_weight[0, 0], (2, 1, 0)),
+        error_scale[None],
         jnp.transpose(jacobian[0, 0], (0, 2, 1, 3)),
     )
-    return (adjoint + error_scale[None, :, None, None] * own)[None]
+    return gradient[None]
 
 
 def solution(mesh):

time: 113 us -> 113 us (level)
  other arithmetic: 2.08 us -> 0 us
  local copies, waits for them, and re-layouts: 0.01 us -> 1.9 us
    broadcast_in_dim x1 -> x0, other arithmetic: 2.08 us -> none  [shards(): return (adjoint + error_scale[None, :, None, None] * own)[None]]
    unnamed x4 -> x1, local copies, waits for them, and re-layouts: 0.01 us -> 1.9 us
where the time goes in v4:
time: 113 us; the launch traced here: 112 us
  Pallas kernels  111 us (98%)
  local copies, waits for them, and re-layouts  1.9 us (2%)
    pallas_call x1, Pallas kernels, run(): pl.pallas_call(functools.partial(whole_loop, bands), out_shape=jax.ShapeD...  111 us

profile of v4, /device:TPU:0, one launch (start us, length us, event | category | flops | bytes accessed | tf_op | source)
XLA Modules:
  0.0 112.4 jit_solution(5643782644560275760)
XLA Ops:
  0.0 110.5 %inner_loop.1 = f32[2,137,4,128]{3,2,1,0:T(4,128)} custom-call(f32[2,137,4,128]{3,2,1,0:T(4,128)} %bitcast.18, f32[137,137]{1,0:T(8,128)} %coupling_hbm.1, f32[4,128]{1,0:T(4,128)} %diff_hbm.1, s32[16,4,32]{2,1,0:T(4,128)} %bitcast.20, f32[16,4,32]{2,1,0:T(4,128)} %bitcast.21, s32[1,32]{1,0:T(1,128)} %bitcast.23, f32[22,16,32]{2,1,0:T(8,128)} %bitcast.19, ...), custom_call_target="tpu_custom_call" | custom-call | tf_op jit(solution)/shard_map/inner_loop/pallas_call | solution.py:464
  110.5 1.9 %copy.11 = f32[1,2,137,4,128]{4,3,2,1,0:T(4,128)} copy(f32[1,2,137,4,128]{4,3,2,1,0:T(4,128)} %bitcast.17) | data formatting | bytes 1122304

commit v5 on v3

--- a/solution.py
+++ b/solution.py
@@ -29,13 +29,6 @@
 def halves(x):
     high = x.astype(BF16)
     return high, (x - high.astype(F32)).astype(BF16)
-
-
-def thirds(x):
-    high = x.astype(BF16)
-    rest = x - high.astype(F32)
-    middle = rest.astype(BF16)
-    return high, middle, (rest - middle.astype(F32)).astype(BF16)
 
 
 def dot3(a, b, dims=NN):
@@ -157,8 +150,6 @@
     def jac_copy(q):
         return pltpu.make_async_copy(jac.at[q], jbuf.at[q], jsem.at[q])
 
-    loop(0, bands, lambda q: jac_copy(q).start())
-
     place_i = band_column(lax.broadcasted_iota(jnp.int32, (REGION, 1), 0))
     column = lax.broadcasted_iota(jnp.int32, (1, REGION), 1)
     order[...] = (place_i == column).astype(F32).astype(BF16)
@@ -168,8 +159,8 @@
         src[v, 136:, :] = jnp.zeros((8, REGION), F32)
         for r in range(4):
             src[v, :levels, r * 128 : (r + 1) * 128] = f[v, :, r, :]
-        x = thirds(src[v])
-        src[v] = dot(x[0], order[...], NT) + (dot(x[1], order[...], NT) + dot(x[2], order[...], NT))
+        x = halves(src[v])
+        src[v] = dot(x[0], order[...], NT) + dot(x[1], order[...], NT)
 
     pl.semaphore_wait(barrier, len(greeted) + bands - 1)
 
@@ -211,6 +202,7 @@
         mixer[s, 1] = low
 
     def ahead_table():
+        loop(0, bands, lambda q: jac_copy(q).start())
         for copy in spreads:
             copy.wait()
         hmat[...] = step_matrix(bands, b, t, dbuf[0], diff[...], dbuf[1])
@@ -430,8 +422,8 @@
     chain(1, (3, 2, 1, 0), [None] * WINDOWS)
     for v in range(2):
         collect(1, v)
-        x = thirds(whole[1, v])
-        end = dot(x[0], order[...]) + (dot(x[1], order[...]) + dot(x[2], order[...]))
+        x = halves(whole[1, v])
+        end = dot(x[0], order[...]) + dot(x[1], order[...])
         for r in range(4):
             out[v, :, r, :] = end[:levels, r * 128 : (r + 1) * 128]
 

time: 113 us -> 113 us (level)
  no operation moved by 1% of the time
where the time goes in v5:
time: 113 us; the launch traced here: 112 us
  Pallas kernels  110 us (97%)
  other arithmetic  2.08 us (2%)
    pallas_call x1, Pallas kernels, run(): pl.pallas_call(functools.partial(whole_loop, bands), out_shape=jax.ShapeD...  110 us

profile of v5, /device:TPU:0, one launch (start us, length us, event | category | flops | bytes accessed | tf_op | source)
XLA Modules:
  0.0 112.5 jit_solution(16506286518670622197)
XLA Ops:
  0.0 0.0 copy-start
  0.0 0.0 copy-start.1
  0.0 110.4 %inner_loop.1 = f32[2,137,4,128]{3,2,1,0:T(4,128)} custom-call(f32[2,137,4,128]{3,2,1,0:T(4,128)} %bitcast.18, f32[137,137]{1,0:T(8,128)} %coupling_hbm.1, f32[4,128]{1,0:T(4,128)} %diff_hbm.1, s32[16,4,32]{2,1,0:T(4,128)} %bitcast.20, f32[16,4,32]{2,1,0:T(4,128)} %bitcast.21, s32[1,32]{1,0:T(1,128)} %bitcast.22, f32[22,16,32]{2,1,0:T(8,128)} %bitcast.19, ...), custom_call_target="tpu_custom_call" | custom-call | tf_op jit(solution)/shard_map/inner_loop/pallas_call | solution.py:454
  110.4 0.0 copy-done
  110.4 0.0 copy-done.1
  110.4 2.1 %add_bitcast_fusion = f32[1,2,137,4,128]{4,3,2,1,0:T(4,128)} fusion(f32[2,137,4,128]{3,2,1,0:T(4,128)} %inner_loop.1, f32[137]{0:T(256)S(1)} %copy-done.1, f32[1,2,137,4,128]{4,3,2,1,0:T(4,128)S(1)} %copy-done), kind=kLoop, calls=%fused_computation | loop fusion | flops 280576 | bytes 1684004 | tf_op jit(solution)/shard_map/broadcast_in_dim | solution.py:505
Async XLA Ops:
  0.0 110.4 %copy-start = (f32[1,2,137,4,128]{4,3,2,1,0:T(4,128)S(1)}, f32[1,2,137,4,128]{4,3,2,1,0:T(4,128)}, u32[]{:S(2)}) copy-start(f32[1,2,137,4,128]{4,3,2,1,0:T(4,128)} %param.9) | copy-start | bytes 1683460
  0.0 110.4 %copy-start.1 = (f32[137]{0:T(256)S(1)}, f32[137]{0:T(256)}, u32[]{:S(2)}) copy-start(f32[137]{0:T(256)} %param.12) | copy-start | bytes 1648
